TPU v7x, 32 devices: a whole 2x2x4 slice. The times are simulated.
32 devices in a mesh: particle: 4 (over z), tile: 8 (over y, x, core).
Axes of the slice: x: 2, y: 2, z: 4, core: 2. Of those that a mesh axis runs over, the one named last changes fastest.
Arguments:
- biomass: float32 [16, 32768], P('particle', 'tile'), as said below
- water: float32 [16, 32768], P('particle', 'tile'), may hold values from -5 to 5
- flow_blocks: bfloat16 [256, 3, 128, 128], P('tile'), may hold values from -0.15625 to 0.15625
- neighbours: int32 [256, 3], P('tile'), may hold values from 0 to 255, as said below
- rain: float32 [4, 16, 32768], P(None, 'particle', 'tile'), may hold values from -4 to 4
- growth_rate: float32 [32768], P('tile'), may hold values from 0.05 to 0.5
- observations: float32 [2, 32768], P(None, 'tile'), may hold values from -5 to 5
- obs_precision: float32 [32768], P('tile'), as said below
- ancestors: int32 [2, 16], replicated, may hold values from 0 to 15
Outputs:
- means: float32 [2, 2, 32768], P(None, None, 'tile')
- biomass_out: float32 [16, 32768], P('particle', 'tile')
- water_out: float32 [16, 32768], P('particle', 'tile')
Inputs may be any that keep to these rules, and one draw needn't show every extreme that they name: `neighbours`: row n lists block n first, then one block 1 to 4 blocks below n and one 1 to 4 blocks above n, each clipped to the grid's ends. `biomass`: every entry lies between 0.5 and 2. `obs_precision`: every entry lies between 0.3 / sqrt(32768) and 3 / sqrt(32768).
All inputs are finite; a program needn't handle non-finite values.
Results may differ from a plain program's by a relative error of at most 0.0019.
Values may be sent and summed in bfloat16 or wider, within the bound.
No kernel may reach another device: no remote copies, remote signals or barrier semaphores. Data moves between devices by JAX's collectives and lax.ppermute only.
A program may use at most 64 MiB of HBM per device.

v0:
```python
import jax
import jax.numpy as jnp
from jax import lax
from jax.sharding import PartitionSpec as P

BLK = 128
CYCLES = 2
DAYS = 2
HALO = 4


def padded(cells, sides, width):
    for axis, dim in sides:
        count = lax.axis_size(axis)
        ends = count - 1
        head = lax.slice_in_dim(cells, 0, width, axis=dim)
        tail = lax.slice_in_dim(cells, cells.shape[dim] - width, cells.shape[dim], axis=dim)
        cells = jnp.concatenate(
            [
                lax.ppermute(tail, axis, [(i, (i + 1) % count) for i in range(ends)]),
                cells,
                lax.ppermute(head, axis, [((i + 1) % count, i) for i in range(ends)]),
            ],
            axis=dim,
        )
    return cells


def body(
    biomass,
    water,
    flow_blocks,
    neighbours,
    rain,
    growth_rate,
    observations,
    obs_precision,
    ancestors,
):
    part_dev = biomass.shape[0]
    cells = biomass.shape[1]
    blocks_dev = cells // BLK
    member = lax.axis_index("particle")
    tile_pos = lax.axis_index("tile")
    local_ids = neighbours - tile_pos * blocks_dev + HALO
    bio, wat = (biomass, water)
    collected = []
    for cycle in range(CYCLES):
        misfit_local = -0.5 * jnp.sum(obs_precision * (bio - observations[cycle]) ** 2, axis=1)
        summed = lax.psum(misfit_local, "tile")
        log_weight = lax.all_gather(summed, "particle", axis=0, tiled=True)
        shifted = jnp.exp(log_weight - jnp.max(log_weight))
        weight = shifted / jnp.sum(shifted)
        my_weight = lax.dynamic_slice_in_dim(weight, member * part_dev, part_dev)
        partial_sums = jnp.stack(
            [jnp.sum(my_weight[:, None] * bio, axis=0), jnp.sum(my_weight[:, None] * wat, axis=0)]
        )
        collected.append(lax.psum(partial_sums, "particle"))
        chosen = ancestors[cycle]
        mine = lax.dynamic_slice_in_dim(chosen, member * part_dev, part_dev)
        piece = (
            lax.all_gather(bio, "particle", axis=0, tiled=True),
            lax.all_gather(wat, "particle", axis=0, tiled=True),
        )
        count = piece[0].shape[0]
        hit = jnp.arange(count, dtype=jnp.int32)[None, :] == mine[:, None]
        bio, wat = tuple(
            (jnp.sum(jnp.where(hit[:, :, None], rows[None], 0.0), axis=1) for rows in piece)
        )
        for day in range(DAYS):
            wb = wat.astype(jnp.bfloat16).reshape(part_dev, blocks_dev, BLK)
            extended = padded(wb, (("tile", 1),), HALO)
            nearby = extended[:, local_ids]
            flux = jnp.einsum(
                "pnkc,nkdc->pnd", nearby, flow_blocks, preferred_element_type=jnp.float32
            ).reshape(part_dev, cells)
            wet = wat * wat / (1.0 + wat * wat)
            new_bio = bio + growth_rate * bio * (wet - 0.4 * bio)
            new_wat = wat + flux + rain[cycle * DAYS + day] - 0.2 * bio * wet
            bio = new_bio
            wat = new_wat
    return (jnp.stack(collected), bio, wat)


def solution(mesh):
    placed = (
        P("particle", "tile"),
        P("particle", "tile"),
        P("tile", None, None, None),
        P("tile", None),
        P(None, "particle", "tile"),
        P("tile"),
        P(None, "tile"),
        P("tile"),
        P(),
    )
    return jax.shard_map(
        body,
        mesh=mesh,
        in_specs=placed,
        out_specs=(P(None, None, "tile"), P("particle", "tile"), P("particle", "tile")),
        check_vma=False,
    )
```

profile of v0, /device:TPU:0, one launch (start us, length us, event | category | flops | bytes accessed | tf_op | source)
XLA Modules:
  0.0 191.6 jit_solution(2245552599224987325)
XLA Ops:
  7.2 0.8 fusion.25
  8.2 15.8 %all-gather = f32[4,4,4096]{2,1,0:T(4,128)S(1)} all-gather(f32[1,4,4096]{2,1,0:T(4,128)} %bitcast.146), channel_id=1, replica_groups=mesh['particle'=4,'tile'=8] {'particle'}, dimensions={0}, use_global_device_ids=true | all-gather | bytes 327680 | tf_op jit(solution)/shard_map/all_gather | solution.py:62
  24.1 0.8 reshape.145
  24.8 14.9 %all-gather.1 = f32[4,4,4096]{2,1,0:T(4,128)S(1)} all-gather(f32[1,4,4096]{2,1,0:T(4,128)} %bitcast.152), channel_id=1, replica_groups=mesh['particle'=4,'tile'=8] {'particle'}, dimensions={0}, use_global_device_ids=true | all-gather | bytes 327680 | tf_op jit(solution)/shard_map/all_gather | solution.py:63
  39.7 0.8 reshape.147
  40.5 1.5 select_reduce_fusion.3
  42.0 1.3 collective-permute-start
  43.3 1.3 collective-permute-start.1
  44.6 0.7 compare_select_fusion
  45.5 0.9 fusion.24
  47.1 1.2 dynamic-slice.2
  49.1 1.3 gather_fusion
  50.4 2.9 %multiply_reduce_fusion.5 = (f32[4]{0:T(128)S(1)}, f32[4]{0:T(128)S(1)}, f32[4,4096]{1,0:T(4,128)}, f32[4,4096]{1,0:T(4,128)}, f32[32,4,128,1]{2,1,3,0:T(4,128)S(1)}) fusion(f32[4,4096]{1,0:T(4,128)} %param.9, f32[4096]{0:T(1024)S(1)} %bitcast.156, f32[4096]{0:T(1024)} %param.16, f32[4096]{0:T(1024)S(1)} %bitcast.155, f32[4,4096]{1,0:T(4,128)S(1)} %get-tuple-element.11, ...), kind=kOutput, calls=%fused_computation.50 | convolution fusion | flops 13058040 | bytes 3768352 | tf_op jit(solution)/shard_map/pnkc,nkdc->pnd/dot_general | solution.py:74
  53.4 0.9 fusion.14
  54.9 4.7 %collective-permute-start.2 = (bf16[4,4,128]{2,0,1:T(4,128)(2,1)}, bf16[4,4,128]{2,0,1:T(4,128)(2,1)S(1)}, u32[]{:S(2)}, u32[]{:S(2)}) collective-permute-start(bf16[4,4,128]{2,0,1:T(4,128)(2,1)} %get-tuple-element.27), channel_id=1, source_target_pairs={{0,1},{1,2},{2,3},{3,4},{4,5},{5,6},{6,7},{8,9},{9,10},{10,11},{11... | collective-permute-start | bytes 12296 | tf_op jit(solution)/shard_map/ppermute | solution.py:20
  59.6 1.3 collective-permute-start.3
  61.0 15.7 %all-reduce.2 = (f32[4]{0:T(128)S(1)}, f32[4]{0:T(128)S(1)}) all-reduce(f32[4]{0:T(128)S(1)} %get-tuple-element.38, f32[4]{0:T(128)S(1)} %get-tuple-element.39), channel_id=1, replica_groups=mesh['particle'=4,'tile'=8] {'tile'}, use_global_device_ids=true, to_apply=%region_10.11 | all-reduce | flops 8 | bytes 64 | tf_op jit(solution)/shard_map/psum | solution.py:50
  77.1 11.5 %all-reduce.4 = (f32[16]{0:T(128)S(1)}, f32[16]{0:T(128)S(1)}) all-reduce(f32[16]{0:T(128)S(1)} %dynamic-update-slice.1, f32[16]{0:T(128)S(1)} %dynamic-update-slice), channel_id=1, replica_groups=mesh['particle'=4,'tile'=8] {'particle'}, use_global_device_ids=true, to_apply=%add.1 | all-reduce | flops 32 | bytes 256
  88.6 0.7 reduce_max.19
  89.3 1.4 fusion.17
  90.7 1.4 broadcast_divide_fusion
  92.0 0.7 reduce_max.18
  92.7 1.4 fusion.16
  94.1 1.4 broadcast_divide_fusion.1
  95.6 0.7 multiply_reduce_fusion.4
  96.3 14.1 %all-gather.2 = f32[4,4,4096]{2,1,0:T(4,128)S(1)} all-gather(f32[1,4,4096]{2,1,0:T(4,128)} %bitcast.145), channel_id=1, replica_groups=mesh['particle'=4,'tile'=8] {'particle'}, dimensions={0}, use_global_device_ids=true | all-gather | bytes 327680 | tf_op jit(solution)/shard_map/all_gather | solution.py:62
  110.4 0.7 dynamic_slice.14
  111.1 0.8 reshape.149
  111.9 0.8 pad_maximum_fusion.2
  112.7 0.7 gather_fusion.1
  113.4 2.1 %multiply_reduce_fusion.1 = (f32[4096]{0:T(1024)S(1)}, f32[4096]{0:T(1024)S(1)}, f32[4,4096]{1,0:T(4,128)S(1)}) fusion(f32[4,4096]{1,0:T(4,128)} %get-tuple-element.21, f32[4]{0:T(128)} %dynamic_slice.14, f32[4,4096]{1,0:T(4,128)} %get-tuple-element.22, f32[4,4096]{1,0:T(4,128)S(1)} %get-tuple-element.11, f32[4,4096]{1,0:T(4,128)S(1)} %get-tuple-element.12, ...), kind=kOutput, calls=%fused_computation.44 | convolution fusion | flops 12902400 | bytes 3686416 | tf_op jit(solution)/shard_map/pnkc,nkdc->pnd/dot_general | solution.py:74
  115.5 13.8 %all-gather.3 = f32[4,4,4096]{2,1,0:T(4,128)S(1)} all-gather(f32[1,4,4096]{2,1,0:T(4,128)S(1)} %bitcast.151), channel_id=1, replica_groups=mesh['particle'=4,'tile'=8] {'particle'}, dimensions={0}, use_global_device_ids=true | all-gather | bytes 327680 | tf_op jit(solution)/shard_map/all_gather | solution.py:63
  129.3 0.8 reshape.151
  130.1 1.5 select_reduce_fusion.1
  131.6 1.3 collective-permute-start.4
  132.9 1.3 collective-permute-start.5
  134.2 1.4 maximum_bitcast_fusion
  135.6 0.9 collective-permute-done.5
  136.5 0.7 gather_fusion.2
  137.2 2.7 %multiply_add_fusion = (f32[4,4096]{1,0:T(4,128)}, f32[4,4096]{1,0:T(4,128)S(1)}, f32[32,4,128,1]{2,1,3,0:T(4,128)S(1)}) fusion(f32[4096]{0:T(1024)S(1)} %copy-done.2, f32[4,4096]{1,0:T(4,128)S(1)} %get-tuple-element.5, f32[4,4096]{1,0:T(4,128)S(1)} %get-tuple-element.6, f32[4,4,4096]{2,1,0:T(4,128)} %param.13, bf16[4,32,3,128]{3,0,2,1:T(4,128)(2,1)S(1)} %bitcast.150, ...), kind=kOutput, calls=%fused_computation.41 | convolution fusion | flops 12926976 | bytes 3653632 | tf_op jit(solution)/shard_map/pnkc,nkdc->pnd/dot_general | solution.py:74
  139.9 0.9 fusion.15
  140.8 4.3 %collective-permute-start.6 = (bf16[4,4,128]{2,0,1:T(4,128)(2,1)S(1)}, bf16[4,4,128]{2,0,1:T(4,128)(2,1)S(1)}, u32[]{:S(2)}, u32[]{:S(2)}) collective-permute-start(bf16[4,4,128]{2,0,1:T(4,128)(2,1)S(1)} %get-tuple-element.23), channel_id=1, source_target_pairs={{0,1},{1,2},{2,3},{3,4},{4,5},{5,6},{6,7},{8,9},{9,10},{10,11},{11... | collective-permute-start | bytes 12296 | tf_op jit(solution)/shard_map/ppermute | solution.py:20
  145.1 1.3 collective-permute-start.7
  147.1 1.8 collective-permute-done.7
  149.0 0.7 gather_fusion.3
  149.7 2.7 %fusion.2 = f32[4,4096]{1,0:T(4,128)} fusion(f32[4,4096]{1,0:T(4,128)S(1)} %get-tuple-element.20, bf16[4,32,3,128]{3,0,2,1:T(4,128)(2,1)S(1)} %bitcast.147, bf16[32,3,128,128]{3,2,1,0:T(8,128)(2,1)S(1)} %copy-done, f32[4,4,4096]{2,1,0:T(4,128)} %param.13, f32[4,4096]{1,0:T(4,128)S(1)} %get-tuple-element.5, f32[4,4096]{1,0:T(4,128)S(1)} %get-tuple-element.6, ...), kind=kOutput, calls=%fused_computation.7 | convolution fusion | flops 12845056 | bytes 3588096 | tf_op jit(solution)/shard_map/pnkc,nkdc->pnd/dot_general | solution.py:74
  152.3 31.0 %all-reduce.7.cloned.1.call-done = (f32[1,2,4096]{2,1,0:T(2,128)}, f32[1,2,4096]{2,1,0:T(2,128)}) async-done(((f32[1,2,4096]{2,1,0:T(2,128)}, f32[1,2,4096]{2,1,0:T(2,128)}), (f32[1,2,4096]{2,1,0:T(2,128)}, f32[1,2,4096]{2,1,0:T(2,128)})) %all-reduce.7.cloned.1.call-update) | async-done | bytes 65552 | tf_op jit(solution)/shard_map/psum | solution.py:58
  183.4 1.4 pad_maximum_fusion
  (43 shorter events, 3.1 us)
Async XLA Ops:
  7.2 43.3 %copy-start = (bf16[32,3,128,128]{3,2,1,0:T(8,128)(2,1)S(1)}, bf16[32,3,128,128]{3,2,1,0:T(8,128)(2,1)}, u32[]{:S(2)}) copy-start(bf16[32,3,128,128]{3,2,1,0:T(8,128)(2,1)} %param.11) | copy-start | bytes 9437188
  7.2 176.2 %all-reduce.7.cloned.1.call-start = ((), (), s32[]{:S(2)}) async-start(), calls=%async_computation | async-start | bytes 131072 | tf_op jit(solution)/shard_map/psum | solution.py:58
  24.8 70.7 %copy-start.1 = (f32[4,4096]{1,0:T(4,128)S(1)}, f32[4,4096]{1,0:T(4,128)}, u32[]{:S(2)}) copy-start(f32[4,4096]{1,0:T(4,128)} %param.9) | copy-start | bytes 196612
  24.8 70.7 %copy-start.3 = (f32[4,4096]{1,0:T(4,128)S(1)}, f32[4,4096]{1,0:T(4,128)}, u32[]{:S(2)}) copy-start(f32[4,4096]{1,0:T(4,128)} %param.10) | copy-start | bytes 196612
  42.0 7.0 %collective-permute-start = (bf16[4,4,128]{2,0,1:T(4,128)(2,1)S(1)}, bf16[4,4,128]{2,0,1:T(4,128)(2,1)S(1)}, u32[]{:S(2)}, u32[]{:S(2)}) collective-permute-start(bf16[4,4,128]{2,0,1:T(4,128)(2,1)S(1)} %get-tuple-element.29), channel_id=1, source_target_pairs={{0,1},{1,2},{2,3},{3,4},{4,5},{5,6},{6,7},{8,9},{9,10},{10,11},{11... | collective-permute-start | bytes 12296 | tf_op jit(solution)/shard_map/ppermute | solution.py:20
  43.3 5.7 %collective-permute-start.1 = (bf16[4,4,128]{2,0,1:T(4,128)(2,1)S(1)}, bf16[4,4,128]{2,0,1:T(4,128)(2,1)S(1)}, u32[]{:S(2)}, u32[]{:S(2)}) collective-permute-start(bf16[4,4,128]{2,0,1:T(4,128)(2,1)S(1)} %get-tuple-element.30), channel_id=1, source_target_pairs={{1,0},{2,1},{3,2},{4,3},{5,4},{6,5},{7,6},{9,8},{10,9},{11,10},{12... | collective-permute-start | bytes 12296 | tf_op jit(solution)/shard_map/ppermute | solution.py:22
  54.3 42.0 %copy-start.4 = (bf16[4,32,128]{2,0,1:T(4,128)(2,1)}, bf16[4,32,128]{2,0,1:T(4,128)(2,1)S(1)}, u32[]{:S(2)}) copy-start(bf16[4,32,128]{2,0,1:T(4,128)(2,1)S(1)} %fusion.14) | copy-start | bytes 98308
  54.9 57.0 %collective-permute-start.2 = (bf16[4,4,128]{2,0,1:T(4,128)(2,1)}, bf16[4,4,128]{2,0,1:T(4,128)(2,1)S(1)}, u32[]{:S(2)}, u32[]{:S(2)}) collective-permute-start(bf16[4,4,128]{2,0,1:T(4,128)(2,1)} %get-tuple-element.27), channel_id=1, source_target_pairs={{0,1},{1,2},{2,3},{3,4},{4,5},{5,6},{6,7},{8,9},{9,10},{10,11},{11... | collective-permute-start | bytes 12296 | tf_op jit(solution)/shard_map/ppermute | solution.py:20
  59.6 52.2 %collective-permute-start.3 = (bf16[4,4,128]{2,0,1:T(4,128)(2,1)}, bf16[4,4,128]{2,0,1:T(4,128)(2,1)}, u32[]{:S(2)}, u32[]{:S(2)}) collective-permute-start(bf16[4,4,128]{2,0,1:T(4,128)(2,1)} %get-tuple-element.28), channel_id=1, source_target_pairs={{1,0},{2,1},{3,2},{4,3},{5,4},{6,5},{7,6},{9,8},{10,9},{11,10},{12... | collective-permute-start | bytes 12296 | tf_op jit(solution)/shard_map/ppermute | solution.py:22
  111.8 22.4 %copy-start.5 = (f32[4096]{0:T(1024)S(1)}, f32[4096]{0:T(1024)}, u32[]{:S(2)}) copy-start(f32[4096]{0:T(1024)} %get-tuple-element.7) | copy-start | bytes 49156
  111.8 25.4 %copy-start.2 = (f32[4096]{0:T(1024)S(1)}, f32[4096]{0:T(1024)}, u32[]{:S(2)}) copy-start(f32[4096]{0:T(1024)} %param.14) | copy-start | bytes 49156
  131.6 4.0 %collective-permute-start.4 = (bf16[4,4,128]{2,0,1:T(4,128)(2,1)S(1)}, bf16[4,4,128]{2,0,1:T(4,128)(2,1)S(1)}, u32[]{:S(2)}, u32[]{:S(2)}) collective-permute-start(bf16[4,4,128]{2,0,1:T(4,128)(2,1)S(1)} %get-tuple-element.25), channel_id=1, source_target_pairs={{0,1},{1,2},{2,3},{3,4},{4,5},{5,6},{6,7},{8,9},{9,10},{10,11},{11... | collective-permute-start | bytes 12296 | tf_op jit(solution)/shard_map/ppermute | solution.py:20
  132.9 3.5 %collective-permute-start.5 = (bf16[4,4,128]{2,0,1:T(4,128)(2,1)S(1)}, bf16[4,4,128]{2,0,1:T(4,128)(2,1)S(1)}, u32[]{:S(2)}, u32[]{:S(2)}) collective-permute-start(bf16[4,4,128]{2,0,1:T(4,128)(2,1)S(1)} %get-tuple-element.26), channel_id=1, source_target_pairs={{1,0},{2,1},{3,2},{4,3},{5,4},{6,5},{7,6},{9,8},{10,9},{11,10},{12... | collective-permute-start | bytes 12296 | tf_op jit(solution)/shard_map/ppermute | solution.py:22
  140.8 6.3 %collective-permute-start.6 = (bf16[4,4,128]{2,0,1:T(4,128)(2,1)S(1)}, bf16[4,4,128]{2,0,1:T(4,128)(2,1)S(1)}, u32[]{:S(2)}, u32[]{:S(2)}) collective-permute-start(bf16[4,4,128]{2,0,1:T(4,128)(2,1)S(1)} %get-tuple-element.23), channel_id=1, source_target_pairs={{0,1},{1,2},{2,3},{3,4},{4,5},{5,6},{6,7},{8,9},{9,10},{10,11},{11... | collective-permute-start | bytes 12296 | tf_op jit(solution)/shard_map/ppermute | solution.py:20
  145.1 3.8 %collective-permute-start.7 = (bf16[4,4,128]{2,0,1:T(4,128)(2,1)S(1)}, bf16[4,4,128]{2,0,1:T(4,128)(2,1)S(1)}, u32[]{:S(2)}, u32[]{:S(2)}) collective-permute-start(bf16[4,4,128]{2,0,1:T(4,128)(2,1)S(1)} %get-tuple-element.24), channel_id=1, source_target_pairs={{1,0},{2,1},{3,2},{4,3},{5,4},{6,5},{7,6},{9,8},{10,9},{11,10},{12... | collective-permute-start | bytes 12296 | tf_op jit(solution)/shard_map/ppermute | solution.py:22
Sparse Core Ops, SparseCore 0:
  147.2 36.1 all-reduce.6
where the time goes:
time: 193 us; the launch traced here: 192 us
  blocking collectives  85.8 us (44%)
  waiting for transfers between devices  33.8 us (18%)
  other arithmetic  18.2 us (9%)
  starting transfers between devices  16.8 us (9%)
  between operations  15 us (8%)
  local copies, waits for them, and re-layouts  11.7 us (6%)
  matrix products  10.5 us (5%)
    psum x1, waiting for transfers between devices, body(): collected.append(lax.psum(partial_sums, 'particle'))  31 us
    all_gather x2, blocking collectives, body(): lax.all_gather(bio, 'particle', axis=0, tiled=True)  29.9 us
    all_gather x2, blocking collectives, body(): lax.all_gather(wat, 'particle', axis=0, tiled=True)  28.7 us
    psum x1, blocking collectives, body(): summed = lax.psum(misfit_local, 'tile')  15.7 us
    ppermute x4, starting transfers between devices, padded(): lax.ppermute(tail, axis, [(i, (i + 1) % count) for i in range(ends)])  11.6 us
    unnamed x1, blocking collectives  11.5 us
    dot_general x4, matrix products, body(): jnp.einsum('pnkc,nkdc->pnd', nearby, flow_blocks, preferred_element_type=...  10.5 us
    ppermute x4, starting transfers between devices, padded(): lax.ppermute(head, axis, [((i + 1) % count, i) for i in range(ends)])  5.17 us
  transfers between devices with their start and end apart: 9, of which 3 were waited for; matrix products, arithmetic and copies ran while one was open for 10% of the time, Pallas kernels for 0%

commit v1 on v0

--- a/solution.py
+++ b/solution.py
@@ -7,6 +7,23 @@
 CYCLES = 2
 DAYS = 2
 HALO = 4
+
+
+def in_order(blocks, dim):
+    blocks = jnp.moveaxis(blocks, 0, dim)
+    dims = blocks.shape
+    return blocks.reshape(*dims[:dim], dims[dim] * dims[dim + 1], *dims[dim + 2 :])
+
+
+def ring_gather(x, axis, dim):
+    devices = lax.axis_size(axis)
+    ahead = [(i, (i + 1) % devices) for i in range(devices)]
+    tiles = [x]
+    while len(tiles) < devices:
+        tiles.append(lax.ppermute(tiles[-1], axis, ahead))
+    here = lax.axis_index(axis)
+    tiles = jnp.stack(tiles)[(here - jnp.arange(devices)) % devices]
+    return in_order(tiles, dim)
 
 
 def padded(cells, sides, width):
@@ -60,7 +77,7 @@
         mine = lax.dynamic_slice_in_dim(chosen, member * part_dev, part_dev)
         piece = (
             lax.all_gather(bio, "particle", axis=0, tiled=True),
-            lax.all_gather(wat, "particle", axis=0, tiled=True),
+            ring_gather(wat, "particle", 0),
         )
         count = piece[0].shape[0]
         hit = jnp.arange(count, dtype=jnp.int32)[None, :] == mine[:, None]

time: 193 us -> 216 us (1.12)
  blocking collectives: 85.8 us -> 54 us
  local copies, waits for them, and re-layouts: 11.7 us -> 34.2 us
  other arithmetic: 18.2 us -> 31 us
  waiting for transfers between devices: 33.8 us -> 45.6 us
  starting transfers between devices: 16.8 us -> 22.8 us
    all_gather x2 -> x0, blocking collectives: 28.7 us -> none  [body(): lax.all_gather(wat, 'particle', axis=0, tiled=True)]
    ppermute x0 -> x6, waiting for transfers between devices: none -> 20.1 us  [ring_gather(): tiles.append(lax.ppermute(tiles[-1], axis, ahead))]
    psum x1, waiting for transfers between devices: 31 us -> 23.7 us  [body(): collected.append(lax.psum(partial_sums, 'particle'))]
    ppermute x0 -> x6, starting transfers between devices: none -> 6.55 us  [ring_gather(): tiles.append(lax.ppermute(tiles[-1], axis, ahead))]
    unnamed x21 -> x29, local copies, waits for them, and re-layouts: 4.85 us -> 10.8 us
    gather x4, local copies, waits for them, and re-layouts: 3.43 us -> 8.44 us  [body(): nearby = extended[:, local_ids]]
    concatenate x4, other arithmetic: 0.92 us -> 5.63 us  [padded(): jnp.concatenate([lax.ppermute(tail, axis, [(i, (i + 1) % count) for i in...]
    gather x0 -> x2, local copies, waits for them, and re-layouts: none -> 4.67 us  [ring_gather(): tiles = jnp.stack(tiles)[(here - jnp.arange(devices)) % devices]]
  transfers between devices with their start and end apart: 9 -> 15, of which waited for: 3 -> 7; matrix products, arithmetic and copies ran while one was open for 10% -> 18% of each run, Pallas kernels for 0% -> 0%
where the time goes in v1:
time: 216 us; the launch traced here: 214 us
  blocking collectives  54 us (25%)
  waiting for transfers between devices  45.6 us (21%)
  local copies, waits for them, and re-layouts  34.2 us (16%)
  other arithmetic  31 us (14%)
  starting transfers between devices  22.8 us (11%)
  between operations  14.8 us (7%)
  matrix products  11.9 us (6%)
    all_gather x2, blocking collectives, body(): lax.all_gather(bio, 'particle', axis=0, tiled=True)  30.2 us
    psum x1, waiting for transfers between devices, body(): collected.append(lax.psum(partial_sums, 'particle'))  23.7 us
    ppermute x6, waiting for transfers between devices, ring_gather(): tiles.append(lax.ppermute(tiles[-1], axis, ahead))  20.1 us
    psum x1, blocking collectives, body(): summed = lax.psum(misfit_local, 'tile')  14.9 us
    dot_general x4, matrix products, body(): jnp.einsum('pnkc,nkdc->pnd', nearby, flow_blocks, preferred_element_type=...  11.9 us
    ppermute x4, starting transfers between devices, padded(): lax.ppermute(tail, axis, [(i, (i + 1) % count) for i in range(ends)])  11.1 us
    unnamed x29, local copies, waits for them, and re-layouts  10.8 us
    unnamed x1, blocking collectives  8.92 us
  transfers between devices with their start and end apart: 15, of which 7 were waited for; matrix products, arithmetic and copies ran while one was open for 18% of the time, Pallas kernels for 0%

profile of v1, /device:TPU:0, one launch (start us, length us, event | category | flops | bytes accessed | tf_op | source)
XLA Modules:
  0.0 214.4 jit_solution(7505295047641305509)
XLA Ops:
  7.2 3.1 %collective-permute-start = (f32[4,4096]{1,0:T(4,128)}, f32[4,4096]{1,0:T(4,128)S(1)}, u32[]{:S(2)}, u32[]{:S(2)}) collective-permute-start(f32[4,4096]{1,0:T(4,128)} %param.10), channel_id=1, source_target_pairs={{0,8},{8,16},{16,24},{24,0},{1,9},{9,17},{17,25},{25,1},{2,10},{10... | collective-permute-start | bytes 196616 | tf_op jit(solution)/shard_map/ppermute | solution.py:23
  11.2 1.5 fusion.35
  14.1 15.0 %all-gather = f32[4,4,4096]{2,1,0:T(4,128)} all-gather(f32[1,4,4096]{2,1,0:T(4,128)} %bitcast.201), channel_id=1, replica_groups=mesh['particle'=4,'tile'=8] {'particle'}, dimensions={0}, use_global_device_ids=true | all-gather | bytes 327680 | tf_op jit(solution)/shard_map/all_gather | solution.py:79
  29.1 1.7 reshape.297
  31.6 6.0 %collective-permute-done.1 = f32[4,4096]{1,0:T(4,128)S(1)} collective-permute-done((f32[4,4096]{1,0:T(4,128)S(1)}, f32[4,4096]{1,0:T(4,128)S(1)}, u32[]{:S(2)}, u32[]{:S(2)}) %collective-permute-start.1) | collective-permute-done | bytes 65568 | tf_op jit(solution)/shard_map/ppermute | solution.py:23
  37.6 6.1 %collective-permute-done.2 = f32[4,4096]{1,0:T(4,128)S(1)} collective-permute-done((f32[4,4096]{1,0:T(4,128)S(1)}, f32[4,4096]{1,0:T(4,128)S(1)}, u32[]{:S(2)}, u32[]{:S(2)}) %collective-permute-start.2) | collective-permute-done | bytes 65568 | tf_op jit(solution)/shard_map/ppermute | solution.py:23
  43.6 1.6 pad_maximum_fusion
  45.2 2.3 %gather_fusion = f32[4,4,4096]{2,1,0:T(4,128)} fusion(f32[4,4,4096]{2,1,0:T(4,128)} %pad_maximum_fusion, s32[1024]{0:T(1024)S(1)} %pad_clamp_fusion.1), kind=kCustom, calls=%fused_computation | custom fusion | bytes 524304 | tf_op jit(solution)/shard_map/gather | solution.py:25
  47.6 1.7 broadcast_in_dim.84
  49.3 1.5 select_reduce_fusion.3
  52.7 1.3 collective-permute-start.4
  56.4 1.3 collective-permute-done.4
  57.7 1.4 pad_maximum_fusion.3
  59.1 2.1 gather_fusion.1
  61.2 2.9 %multiply_reduce_fusion.5 = (f32[4]{0:T(128)S(1)}, f32[4]{0:T(128)S(1)}, f32[4,4096]{1,0:T(4,128)}, f32[4,4096]{1,0:T(4,128)}, f32[32,4,128,1]{2,1,3,0:T(4,128)S(1)}) fusion(f32[4,4096]{1,0:T(4,128)} %param.9, f32[4096]{0:T(1024)} %bitcast.208, f32[4096]{0:T(1024)} %param.16, f32[4096]{0:T(1024)} %bitcast.207, f32[4,4096]{1,0:T(4,128)S(1)} %get-tuple-element.11, ...), kind=kOutput, calls=%fused_computation.71 | convolution fusion | flops 13058040 | bytes 3768352 | tf_op jit(solution)/shard_map/pnkc,nkdc->pnd/dot_general | solution.py:91
  66.1 4.3 %collective-permute-start.5 = (bf16[4,4,128]{2,0,1:T(4,128)(2,1)}, bf16[4,4,128]{2,0,1:T(4,128)(2,1)S(1)}, u32[]{:S(2)}, u32[]{:S(2)}) collective-permute-start(bf16[4,4,128]{2,0,1:T(4,128)(2,1)} %get-tuple-element.28), channel_id=1, source_target_pairs={{0,1},{1,2},{2,3},{3,4},{4,5},{5,6},{6,7},{8,9},{9,10},{10,11},{11... | collective-permute-start | bytes 12296 | tf_op jit(solution)/shard_map/ppermute | solution.py:37
  72.2 14.9 %all-reduce.2 = (f32[4]{0:T(128)}, f32[4]{0:T(128)}) all-reduce(f32[4]{0:T(128)} %get-tuple-element.39, f32[4]{0:T(128)} %get-tuple-element.40), channel_id=1, replica_groups=mesh['particle'=4,'tile'=8] {'tile'}, use_global_device_ids=true, to_apply=%region_10.11 | all-reduce | flops 8 | bytes 64 | tf_op jit(solution)/shard_map/psum | solution.py:67
  87.7 1.3 dynamic-update-slice
  90.8 8.9 %all-reduce.4 = (f32[16]{0:T(128)}, f32[16]{0:T(128)}) all-reduce(f32[16]{0:T(128)} %dynamic-update-slice.1, f32[16]{0:T(128)} %dynamic-update-slice), channel_id=1, replica_groups=mesh['particle'=4,'tile'=8] {'particle'}, use_global_device_ids=true, to_apply=%add.1 | all-reduce | flops 32 | bytes 256
  100.9 1.9 fusion.27
  102.8 2.4 %broadcast_divide_fusion = f32[16]{0:T(128)} fusion(f32[]{:T(128)} %fusion.27, f32[16]{0:T(128)} %get-tuple-element.17, f32[]{:T(128)} %reduce_max.19), kind=kLoop, calls=%fused_computation.95 | loop fusion | flops 32 | bytes 136 | tf_op jit(solution)/shard_map/div | solution.py:70
  106.5 1.8 fusion.26
  108.3 1.9 broadcast_divide_fusion.1
  110.3 1.6 multiply_reduce_fusion.4
  111.9 1.3 dynamic_slice.14
  113.2 1.4 pad_maximum_fusion.4
  114.6 2.1 gather_fusion.2
  116.7 3.4 %multiply_reduce_fusion.1 = (f32[4096]{0:T(1024)}, f32[4096]{0:T(1024)}, f32[4,4096]{1,0:T(4,128)S(1)}, f32[32,4,128,1]{2,1,3,0:T(4,128)}) fusion(f32[4,4096]{1,0:T(4,128)} %get-tuple-element.22, f32[4]{0:T(128)} %dynamic_slice.14, f32[4,4096]{1,0:T(4,128)} %get-tuple-element.23, f32[4,4096]{1,0:T(4,128)S(1)} %get-tuple-element.11, ...), kind=kOutput, calls=%fused_computation.65 | convolution fusion | flops 12902400 | bytes 3751952 | tf_op jit(solution)/shard_map/pnkc,nkdc->pnd/dot_general | solution.py:91
  120.2 2.0 collective-permute-start.7
  122.8 3.6 %collective-permute-done.7 = f32[4,4096]{1,0:T(4,128)} collective-permute-done((f32[4,4096]{1,0:T(4,128)S(1)}, f32[4,4096]{1,0:T(4,128)}, u32[]{:S(2)}, u32[]{:S(2)}) %collective-permute-start.7) | collective-permute-done | bytes 65568 | tf_op jit(solution)/shard_map/ppermute | solution.py:23
  127.0 15.1 %all-gather.1 = f32[4,4,4096]{2,1,0:T(4,128)} all-gather(f32[1,4,4096]{2,1,0:T(4,128)S(1)} %bitcast.200), channel_id=1, replica_groups=mesh['particle'=4,'tile'=8] {'particle'}, dimensions={0}, use_global_device_ids=true | all-gather | bytes 327680 | tf_op jit(solution)/shard_map/all_gather | solution.py:79
  142.2 1.7 reshape.299
  145.7 4.5 %collective-permute-done.9 = f32[4,4096]{1,0:T(4,128)S(1)} collective-permute-done((f32[4,4096]{1,0:T(4,128)}, f32[4,4096]{1,0:T(4,128)S(1)}, u32[]{:S(2)}, u32[]{:S(2)}) %collective-permute-start.9) | collective-permute-done | bytes 65568 | tf_op jit(solution)/shard_map/ppermute | solution.py:23
  150.2 1.6 pad_maximum_fusion.1
  151.8 2.3 %gather_fusion.3 = f32[4,4,4096]{2,1,0:T(4,128)} fusion(f32[4,4,4096]{2,1,0:T(4,128)} %pad_maximum_fusion.1, s32[1024]{0:T(1024)S(1)} %pad_clamp_fusion.1), kind=kCustom, calls=%fused_computation.3 | custom fusion | bytes 524304 | tf_op jit(solution)/shard_map/gather | solution.py:25
  154.2 1.7 broadcast_in_dim.89
  155.9 1.5 select_reduce_fusion.1
  159.9 1.3 collective-permute-start.11
  161.2 1.4 maximum_bitcast_fusion.1
  163.0 1.4 pad_maximum_fusion.5
  164.4 2.1 gather_fusion.4
  166.5 2.8 %multiply_add_fusion = (f32[4,4096]{1,0:T(4,128)}, f32[4,4096]{1,0:T(4,128)}, f32[32,4,128,1]{2,1,3,0:T(4,128)S(1)}) fusion(f32[4096]{0:T(1024)} %param.14, f32[4,4096]{1,0:T(4,128)S(1)} %get-tuple-element.5, f32[4,4096]{1,0:T(4,128)S(1)} %get-tuple-element.6, f32[4,4,4096]{2,1,0:T(4,128)S(1)} %copy-done.1, bf16[4,32,3,128]{3,0,2,1:T(4,128)(2,1)} %bitcast.205, ...), kind=kOutput, calls=%fused_computation.62 | convolution fusion | flops 12926976 | bytes 3653632 | tf_op jit(solution)/shard_map/pnkc,nkdc->pnd/dot_general | solution.py:91
  170.5 4.3 %collective-permute-start.12 = (bf16[4,4,128]{2,0,1:T(4,128)(2,1)}, bf16[4,4,128]{2,0,1:T(4,128)(2,1)S(1)}, u32[]{:S(2)}, u32[]{:S(2)}) collective-permute-start(bf16[4,4,128]{2,0,1:T(4,128)(2,1)} %get-tuple-element.24), channel_id=1, source_target_pairs={{0,1},{1,2},{2,3},{3,4},{4,5},{5,6},{6,7},{8,9},{9,10},{10,11},{11... | collective-permute-start | bytes 12296 | tf_op jit(solution)/shard_map/ppermute | solution.py:37
  176.1 23.7 %all-reduce.7.cloned.1.call-done = (f32[1,2,4096]{2,1,0:T(2,128)}, f32[1,2,4096]{2,1,0:T(2,128)}) async-done(((f32[1,2,4096]{2,1,0:T(2,128)}, f32[1,2,4096]{2,1,0:T(2,128)}), (f32[1,2,4096]{2,1,0:T(2,128)}, f32[1,2,4096]{2,1,0:T(2,128)})) %all-reduce.7.cloned.1.call-update) | async-done | bytes 65552 | tf_op jit(solution)/shard_map/psum | solution.py:75
  199.8 1.4 pad_maximum_fusion.2
  201.2 1.4 pad_maximum_fusion.6
  202.7 2.1 gather_fusion.5
  204.8 2.8 %fusion.2 = f32[4,4096]{1,0:T(4,128)} fusion(f32[4,4096]{1,0:T(4,128)} %get-tuple-element.20, bf16[4,32,3,128]{3,0,2,1:T(4,128)(2,1)} %bitcast.202, bf16[32,3,128,128]{3,2,1,0:T(8,128)(2,1)S(1)} %copy-done, f32[4,4,4096]{2,1,0:T(4,128)S(1)} %copy-done.1, f32[4,4096]{1,0:T(4,128)S(1)} %get-tuple-element.5, f32[4,4096]{1,0:T(4,128)S(1)} %get-tuple-element.6, ...), kind=kOutput, calls=%fused_computation.9 | convolution fusion | flops 12845056 | bytes 3588096 | tf_op jit(solution)/shard_map/pnkc,nkdc->pnd/dot_general | solution.py:91
  (70 shorter events, 23.9 us)
Async XLA Ops:
  7.2 54.1 %copy-start = (bf16[32,3,128,128]{3,2,1,0:T(8,128)(2,1)S(1)}, bf16[32,3,128,128]{3,2,1,0:T(8,128)(2,1)}, u32[]{:S(2)}) copy-start(bf16[32,3,128,128]{3,2,1,0:T(8,128)(2,1)} %param.11) | copy-start | bytes 9437188
  7.2 54.1 %copy-start.1 = (f32[4,4,4096]{2,1,0:T(4,128)S(1)}, f32[4,4,4096]{2,1,0:T(4,128)}, u32[]{:S(2)}) copy-start(f32[4,4,4096]{2,1,0:T(4,128)} %param.13) | copy-start | bytes 786436
  7.2 192.6 %all-reduce.7.cloned.1.call-start = ((), (), s32[]{:S(2)}) async-start(), calls=%async_computation | async-start | bytes 131072 | tf_op jit(solution)/shard_map/psum | solution.py:75
  7.2 24.3 %collective-permute-start = (f32[4,4096]{1,0:T(4,128)}, f32[4,4096]{1,0:T(4,128)S(1)}, u32[]{:S(2)}, u32[]{:S(2)}) collective-permute-start(f32[4,4096]{1,0:T(4,128)} %param.10), channel_id=1, source_target_pairs={{0,8},{8,16},{16,24},{24,0},{1,9},{9,17},{17,25},{25,1},{2,10},{10... | collective-permute-start | bytes 196616 | tf_op jit(solution)/shard_map/ppermute | solution.py:23
  31.5 6.1 %collective-permute-start.1 = (f32[4,4096]{1,0:T(4,128)S(1)}, f32[4,4096]{1,0:T(4,128)S(1)}, u32[]{:S(2)}, u32[]{:S(2)}) collective-permute-start(f32[4,4096]{1,0:T(4,128)S(1)} %collective-permute-done), channel_id=1, source_target_pairs={{0,8},{8,16},{16,24},{24,0},{1,9},{9,17},{17,25},{25,1},{2,10},{10... | collective-permute-start | bytes 196616 | tf_op jit(solution)/shard_map/ppermute | solution.py:23
  37.6 6.1 %collective-permute-start.2 = (f32[4,4096]{1,0:T(4,128)S(1)}, f32[4,4096]{1,0:T(4,128)S(1)}, u32[]{:S(2)}, u32[]{:S(2)}) collective-permute-start(f32[4,4096]{1,0:T(4,128)S(1)} %collective-permute-done.1), channel_id=1, source_target_pairs={{0,8},{8,16},{16,24},{24,0},{1,9},{9,17},{17,25},{25,1},{2,10},{10... | collective-permute-start | bytes 196616 | tf_op jit(solution)/shard_map/ppermute | solution.py:23
  50.8 1.9 copy-start.5
  51.4 4.9 %collective-permute-start.3 = (bf16[4,4,128]{2,0,1:T(4,128)(2,1)}, bf16[4,4,128]{2,0,1:T(4,128)(2,1)S(1)}, u32[]{:S(2)}, u32[]{:S(2)}) collective-permute-start(bf16[4,4,128]{2,0,1:T(4,128)(2,1)} %get-tuple-element.30), channel_id=1, source_target_pairs={{0,1},{1,2},{2,3},{3,4},{4,5},{5,6},{6,7},{8,9},{9,10},{10,11},{11... | collective-permute-start | bytes 12296 | tf_op jit(solution)/shard_map/ppermute | solution.py:37
  52.7 5.0 %collective-permute-start.4 = (bf16[4,4,128]{2,0,1:T(4,128)(2,1)}, bf16[4,4,128]{2,0,1:T(4,128)(2,1)S(1)}, u32[]{:S(2)}, u32[]{:S(2)}) collective-permute-start(bf16[4,4,128]{2,0,1:T(4,128)(2,1)} %get-tuple-element.31), channel_id=1, source_target_pairs={{1,0},{2,1},{3,2},{4,3},{5,4},{6,5},{7,6},{9,8},{10,9},{11,10},{12... | collective-permute-start | bytes 12296 | tf_op jit(solution)/shard_map/ppermute | solution.py:39
  64.2 0.6 copy-start.3
  64.9 0.6 copy-start.4
  66.1 47.1 %collective-permute-start.5 = (bf16[4,4,128]{2,0,1:T(4,128)(2,1)}, bf16[4,4,128]{2,0,1:T(4,128)(2,1)S(1)}, u32[]{:S(2)}, u32[]{:S(2)}) collective-permute-start(bf16[4,4,128]{2,0,1:T(4,128)(2,1)} %get-tuple-element.28), channel_id=1, source_target_pairs={{0,1},{1,2},{2,3},{3,4},{4,5},{5,6},{6,7},{8,9},{9,10},{10,11},{11... | collective-permute-start | bytes 12296 | tf_op jit(solution)/shard_map/ppermute | solution.py:37
  70.3 42.9 %collective-permute-start.6 = (bf16[4,4,128]{2,0,1:T(4,128)(2,1)}, bf16[4,4,128]{2,0,1:T(4,128)(2,1)S(1)}, u32[]{:S(2)}, u32[]{:S(2)}) collective-permute-start(bf16[4,4,128]{2,0,1:T(4,128)(2,1)} %get-tuple-element.29), channel_id=1, source_target_pairs={{1,0},{2,1},{3,2},{4,3},{5,4},{6,5},{7,6},{9,8},{10,9},{11,10},{12... | collective-permute-start | bytes 12296 | tf_op jit(solution)/shard_map/ppermute | solution.py:39
  116.7 5.4 %copy-start.8 = (f32[4096]{0:T(1024)S(1)}, f32[4096]{0:T(1024)}, u32[]{:S(2)}) copy-start(f32[4096]{0:T(1024)} %get-tuple-element.7) | copy-start | bytes 49156
  116.7 5.4 %copy-start.9 = (f32[4096]{0:T(1024)S(1)}, f32[4096]{0:T(1024)}, u32[]{:S(2)}) copy-start(f32[4096]{0:T(1024)} %get-tuple-element.8) | copy-start | bytes 49156
  116.7 10.3 %copy-start.2 = (f32[4,4096]{1,0:T(4,128)S(1)}, f32[4,4096]{1,0:T(4,128)}, u32[]{:S(2)}) copy-start(f32[4,4096]{1,0:T(4,128)} %get-tuple-element.22) | copy-start | bytes 196612
  116.7 39.1 %copy-start.10 = (pred[4,16]{1,0:T(4,128)(4,1)S(1)}, pred[4,16]{1,0:T(4,128)(4,1)}, u32[]{:S(2)}) copy-start(pred[4,16]{1,0:T(4,128)(4,1)} %iota_compare_fusion) | copy-start | bytes 196
  120.2 6.2 %collective-permute-start.7 = (f32[4,4096]{1,0:T(4,128)S(1)}, f32[4,4096]{1,0:T(4,128)}, u32[]{:S(2)}, u32[]{:S(2)}) collective-permute-start(f32[4,4096]{1,0:T(4,128)S(1)} %get-tuple-element.21), channel_id=1, source_target_pairs={{0,8},{8,16},{16,24},{24,0},{1,9},{9,17},{17,25},{25,1},{2,10},{10... | collective-permute-start | bytes 196616 | tf_op jit(solution)/shard_map/ppermute | solution.py:23
  126.4 17.5 %collective-permute-start.8 = (f32[4,4096]{1,0:T(4,128)}, f32[4,4096]{1,0:T(4,128)}, u32[]{:S(2)}, u32[]{:S(2)}) collective-permute-start(f32[4,4096]{1,0:T(4,128)} %collective-permute-done.7), channel_id=1, source_target_pairs={{0,8},{8,16},{16,24},{24,0},{1,9},{9,17},{17,25},{25,1},{2,10},{10... | collective-permute-start | bytes 196616 | tf_op jit(solution)/shard_map/ppermute | solution.py:23
  143.9 6.3 %collective-permute-start.9 = (f32[4,4096]{1,0:T(4,128)}, f32[4,4096]{1,0:T(4,128)S(1)}, u32[]{:S(2)}, u32[]{:S(2)}) collective-permute-start(f32[4,4096]{1,0:T(4,128)} %collective-permute-done.8), channel_id=1, source_target_pairs={{0,8},{8,16},{16,24},{24,0},{1,9},{9,17},{17,25},{25,1},{2,10},{10... | collective-permute-start | bytes 196616 | tf_op jit(solution)/shard_map/ppermute | solution.py:23
  157.4 0.6 copy-start.6
  158.6 4.0 %collective-permute-start.10 = (bf16[4,4,128]{2,0,1:T(4,128)(2,1)}, bf16[4,4,128]{2,0,1:T(4,128)(2,1)S(1)}, u32[]{:S(2)}, u32[]{:S(2)}) collective-permute-start(bf16[4,4,128]{2,0,1:T(4,128)(2,1)} %get-tuple-element.26), channel_id=1, source_target_pairs={{0,1},{1,2},{2,3},{3,4},{4,5},{5,6},{6,7},{8,9},{9,10},{10,11},{11... | collective-permute-start | bytes 12296 | tf_op jit(solution)/shard_map/ppermute | solution.py:37
  159.9 3.1 %collective-permute-start.11 = (bf16[4,4,128]{2,0,1:T(4,128)(2,1)S(1)}, bf16[4,4,128]{2,0,1:T(4,128)(2,1)S(1)}, u32[]{:S(2)}, u32[]{:S(2)}) collective-permute-start(bf16[4,4,128]{2,0,1:T(4,128)(2,1)S(1)} %get-tuple-element.27), channel_id=1, source_target_pairs={{1,0},{2,1},{3,2},{4,3},{5,4},{6,5},{7,6},{9,8},{10,9},{11,10},{12... | collective-permute-start | bytes 12296 | tf_op jit(solution)/shard_map/ppermute | solution.py:39
  169.3 0.6 copy-start.7
  170.5 30.7 %collective-permute-start.12 = (bf16[4,4,128]{2,0,1:T(4,128)(2,1)}, bf16[4,4,128]{2,0,1:T(4,128)(2,1)S(1)}, u32[]{:S(2)}, u32[]{:S(2)}) collective-permute-start(bf16[4,4,128]{2,0,1:T(4,128)(2,1)} %get-tuple-element.24), channel_id=1, source_target_pairs={{0,1},{1,2},{2,3},{3,4},{4,5},{5,6},{6,7},{8,9},{9,10},{10,11},{11... | collective-permute-start | bytes 12296 | tf_op jit(solution)/shard_map/ppermute | solution.py:37
  174.8 26.5 %collective-permute-start.13 = (bf16[4,4,128]{2,0,1:T(4,128)(2,1)S(1)}, bf16[4,4,128]{2,0,1:T(4,128)(2,1)S(1)}, u32[]{:S(2)}, u32[]{:S(2)}) collective-permute-start(bf16[4,4,128]{2,0,1:T(4,128)(2,1)S(1)} %get-tuple-element.25), channel_id=1, source_target_pairs={{1,0},{2,1},{3,2},{4,3},{5,4},{6,5},{7,6},{9,8},{10,9},{11,10},{12... | collective-permute-start | bytes 12296 | tf_op jit(solution)/shard_map/ppermute | solution.py:39
Sparse Core Ops, SparseCore 0:
  162.7 37.0 all-reduce.6
